TPU v7x, 128 devices: a whole 4x4x4 slice. The times are simulated.
128 devices in a mesh: fsdp: 16 (over x, z_hi, core), rep: 8 (over y, z_lo).
Axes of the slice: x: 4, y: 4, z: 4 (z_hi: 2, z_lo: 2; z = z_hi * 2 + z_lo), core: 2. Of those that a mesh axis runs over, the one named last changes fastest.
Arguments:
- tokens: bfloat16 [65536, 1536], P(('fsdp', 'rep')), may hold values from -6 to 6
- weight: float32 [6144, 1536], P('fsdp'), may hold values from -0.15625 to 0.15625
- cotangent: bfloat16 [65536, 6144], P(('fsdp', 'rep')), may hold values from -24 to 24
Outputs:
- activated: bfloat16 [65536, 6144], P(('fsdp', 'rep'))
- input_grad: float32 [65536, 1536], P(('fsdp', 'rep'))
- weight_grad: float32 [6144, 1536], P('fsdp')
All inputs are finite; a program needn't handle non-finite values.
Results may differ from a plain program's by a relative error of at most 0.022.
Values may be sent and summed in bfloat16 or wider, within the bound.
No kernel may reach another device: no remote copies, remote signals or barrier semaphores. Data moves between devices by JAX's collectives and lax.ppermute only.
A program may use at most 192 MiB of HBM per device.

v0:
```python
import math

import jax
import jax.numpy as jnp
from jax import lax
from jax.sharding import PartitionSpec as P


def gelu_tanh(value):
    return jax.nn.gelu(value, approximate=True)


def hidden_part(tokens, rows, cot_cols):
    pre = lax.dot_general(
        tokens, rows, (((1,), (1,)), ((), ())), preferred_element_type=jnp.float32
    )
    activated, pullback = jax.vjp(gelu_tanh, pre)
    slope_grad = pullback(cot_cols.astype(jnp.float32))[0].astype(jnp.bfloat16)
    return (activated.astype(jnp.bfloat16), slope_grad)


def local(tokens, weight, cotangent):
    weight_b = weight.astype(jnp.bfloat16)
    tok_rows = tokens.shape[0]
    total_tokens = tok_rows * lax.axis_size("fsdp") * lax.axis_size("rep")
    scale = jnp.float32(1.0 / math.sqrt(total_tokens))
    full_rows = lax.all_gather(weight_b, "fsdp", axis=0, tiled=True)
    activated, slope_grad = hidden_part(tokens, full_rows, cotangent)
    input_grad = jnp.dot(slope_grad, full_rows, preferred_element_type=jnp.float32)
    shard_grad = lax.psum_scatter(
        (
            lax.dot_general(
                slope_grad, tokens, (((0,), (0,)), ((), ())), preferred_element_type=jnp.float32
            )
            * scale
        ).astype(jnp.bfloat16),
        "fsdp",
        scatter_dimension=0,
        tiled=True,
    )
    weight_grad = lax.psum(shard_grad, "rep").astype(jnp.float32)
    return (activated, input_grad, weight_grad)


def solution(mesh):
    in_specs = (P(("fsdp", "rep"), None), P("fsdp", None), P(("fsdp", "rep"), None))
    out_specs = (P(("fsdp", "rep"), None), P(("fsdp", "rep"), None), P("fsdp", None))
    return jax.shard_map(local, mesh=mesh, in_specs=in_specs, out_specs=out_specs, check_vma=False)
```

profile of v0, /device:TPU:0, one launch (start us, length us, event | category | flops | bytes accessed | tf_op | source)
XLA Modules:
  0.0 418.1 jit_solution(15677039304942279899)
XLA Ops:
  7.2 0.0 copy-start
  7.2 0.0 all-gather.2.cloned.1.call-start
  7.2 2.9 convert_element_type.18
  10.1 0.0 all-gather.2.cloned.1.call-update
  10.2 0.0 reduce-scatter.2.cloned.1.call-start
  10.2 123.2 %all-gather.2.cloned.1.call-done = bf16[6144,1536]{1,0:T(8,128)(2,1)} async-done(((bf16[384,1536]{1,0:T(8,128)(2,1)}), bf16[6144,1536]{1,0:T(8,128)(2,1)}) %all-gather.2.cloned.1.call-update) | async-done | bytes 18874384 | tf_op jit(solution)/shard_map/all_gather | solution.py:27
  133.4 0.0 copy-done
  133.4 22.9 %fusion.2 = (bf16[512,6144]{1,0:T(8,128)(2,1)S(1)}, bf16[512,6144]{1,0:T(8,128)(2,1)}) fusion(bf16[512,6144]{1,0:T(8,128)(2,1)} %param.5, bf16[512,1536]{1,0:T(8,128)(2,1)S(1)} %copy-done, bf16[6144,1536]{1,0:T(8,128)(2,1)} %all-gather.2.cloned.1.call-done), kind=kOutput, calls=%fused_computation.7 | convolution fusion | flops 9736028160 | bytes 39321600 | tf_op jit(solution)/shard_map/dot_general | solution.py:14
  156.3 0.0 copy-start.2
  156.3 2.6 copy-done.2
  159.0 13.2 %multiply_convert_fusion = bf16[6144,1536]{1,0:T(8,128)(2,1)} fusion(bf16[512,6144]{1,0:T(8,128)(2,1)S(1)} %get-tuple-element.3, bf16[512,1536]{1,0:T(8,128)(2,1)S(1)} %copy-done), kind=kOutput, calls=%fused_computation | convolution fusion | flops 9682550784 | bytes 26738688 | tf_op jit(solution)/shard_map/dot_general | solution.py:32
  172.2 0.0 reduce-scatter.2.cloned.1.call-update
  172.2 0.2 all-reduce.2.cloned.1.call-start
  172.5 156.6 %reduce-scatter.2.cloned.1.call-done = bf16[384,1536]{1,0:T(8,128)(2,1)} async-done(((bf16[6144,1536]{1,0:T(8,128)(2,1)}), bf16[384,1536]{1,0:T(8,128)(2,1)}) %reduce-scatter.2.cloned.1.call-update) | async-done | bytes 1179664 | tf_op jit(solution)/shard_map/reduce_scatter | solution.py:30
  329.1 0.0 all-reduce.2.cloned.1.call-update
  329.1 0.0 copy-start.1
  329.1 16.8 %fusion.10 = f32[512,1536]{1,0:T(8,128)} fusion(bf16[512,6144]{1,0:T(8,128)(2,1)} %copy-done.2, bf16[6144,1536]{1,0:T(8,128)(2,1)} %all-gather.2.cloned.1.call-done), kind=kOutput, calls=%fused_computation.16 | convolution fusion | flops 9663676416 | bytes 28311552 | tf_op jit(solution)/shard_map/dot_general | solution.py:29
  345.9 62.7 %all-reduce.2.cloned.1.call-done = bf16[384,1536]{1,0:T(8,128)(2,1)} async-done(((bf16[384,1536]{1,0:T(8,128)(2,1)}), bf16[384,1536]{1,0:T(8,128)(2,1)}) %all-reduce.2.cloned.1.call-update) | async-done | bytes 1179664 | tf_op jit(solution)/shard_map/psum | solution.py:41
  408.6 3.0 convert_element_type.23
  411.6 0.0 copy-done.1
Async XLA Ops:
  7.2 126.3 %copy-start = (bf16[512,1536]{1,0:T(8,128)(2,1)S(1)}, bf16[512,1536]{1,0:T(8,128)(2,1)}, u32[]{:S(2)}) copy-start(bf16[512,1536]{1,0:T(8,128)(2,1)} %param.3) | copy-start | bytes 4718596
  7.2 126.3 %all-gather.2.cloned.1.call-start = ((), (), s32[]{:S(2)}) async-start(), calls=%async_computation.1 | async-start | bytes 20054016 | tf_op jit(solution)/shard_map/all_gather | solution.py:27
  10.2 318.9 %reduce-scatter.2.cloned.1.call-start = ((), (), s32[]{:S(2)}) async-start(), calls=%async_computation.2 | async-start | bytes 20054016 | tf_op jit(solution)/shard_map/reduce_scatter | solution.py:30
  156.3 2.6 copy-start.2
  172.2 236.4 %all-reduce.2.cloned.1.call-start = ((), (), s32[]{:S(2)}) async-start(), calls=%async_computation.3 | async-start | bytes 2359296 | tf_op jit(solution)/shard_map/psum | solution.py:41
  329.1 82.5 %copy-start.1 = (bf16[512,1536]{1,0:T(8,128)(2,1)S(1)}, bf16[512,1536]{1,0:T(8,128)(2,1)}, u32[]{:S(2)}) copy-start(bf16[512,1536]{1,0:T(8,128)(2,1)} %param.3) | copy-start | bytes 4718596
Sparse Core Ops, SparseCore 0:
  11.0 122.3 all-gather.1
  172.4 156.7 reduce-scatter.1
  331.8 76.8 all-reduce.1
where the time goes:
time: 418 us
  waiting for transfers between devices  343 us (82%)
  matrix products  52.9 us (13%)
  between operations  13.8 us (3%)
  other arithmetic  5.88 us (1%)
    reduce_scatter x1, waiting for transfers between devices, local(): lax.psum_scatter((lax.dot_general(slope_grad, tokens, (((0,), (0,)), ((),...  157 us
    all_gather x1, waiting for transfers between devices, local(): full_rows = lax.all_gather(weight_b, 'fsdp', axis=0, tiled=True)  123 us
    psum x1, waiting for transfers between devices, local(): weight_grad = lax.psum(shard_grad, 'rep').astype(jnp.float32)  62.7 us
    dot_general x1, matrix products, hidden_part(): lax.dot_general(tokens, rows, (((1,), (1,)), ((), ())), preferred_element...  22.9 us
    dot_general x1, matrix products, local(): jnp.dot(slope_grad, full_rows, preferred_element_type=jnp.float32)  16.8 us
    dot_general x1, matrix products, local(): lax.dot_general(slope_grad, tokens, (((0,), (0,)), ((), ())), preferred_e...  13.2 us
  transfers between devices with their start and end apart: 3, of which 3 were waited for; matrix products, arithmetic and copies ran while one was open for 4% of the time, Pallas kernels for 0%

commit v1 on v0

v1 whole, which is shorter than its diff:
```python
import functools
import math

import jax
import jax.numpy as jnp
from jax import lax
from jax.experimental import pallas as pl
from jax.experimental.pallas import tpu as pltpu
from jax.sharding import PartitionSpec as P

BF = jnp.bfloat16
F32 = jnp.float32
NX, NY = 4, 4
TILE = 256
ROLES = ("own", "a", "b", "own_z", "ab", "a_z", "b_z", "ab_z")


def coords(f, r):
    return f // 4, r // 2, (f // 2) % 2, r % 2, f % 2


def permute(value, target):
    pairs = []
    for i in range(128):
        x, y, zh, zl, c = target(*coords(i // 8, i % 8))
        pairs.append((i, (x * 4 + zh * 2 + c) * 8 + y * 2 + zl))
    return lax.ppermute(value, ("fsdp", "rep"), pairs)


def first(i, c):
    return i ^ 1 if c == 0 else 3 - i


def second(i, c):
    return first(i, 1 - c)


def x_first(v):
    return permute(v, lambda x, y, zh, zl, c: (first(x, c), y, zh, zl, c))


def x_second(v):
    return permute(v, lambda x, y, zh, zl, c: (second(x, c), y, zh, zl, c))


def y_first(v):
    return permute(v, lambda x, y, zh, zl, c: (x, first(y, c), zh, zl, c))


def y_second(v):
    return permute(v, lambda x, y, zh, zl, c: (x, second(y, c), zh, zl, c))


def z_outer(v):
    return permute(v, lambda x, y, zh, zl, c: (x, y, 1 - zh, 1 - zl, c))


def z_inner(v):
    return permute(v, lambda x, y, zh, zl, c: (x, y, zh, 1 - zl, c))


def other_core(v):
    return permute(v, lambda x, y, zh, zl, c: (x, y, zh, zl, 1 - c))


def add(a, b):
    return (a.astype(F32) + b.astype(F32)).astype(BF)


def rows_of(v, part, parts):
    n = v.shape[0] // parts
    return lax.dynamic_slice_in_dim(v, part * n, n, 0)


def block_kernel(halves, scale, n_alias, at, tok_o, tok_p, *refs):
    n_w = 2 if halves else 1
    w_in = refs[:n_w]
    cot_o, cot_p = refs[n_w : n_w + 2]
    act_o, act_p, slope_o, w_o, send_o, keep_o, acc = refs[n_w + 2 + n_alias :]
    i = pl.program_id(0)
    n_own = pl.num_programs(0) // 2

    @pl.when(i == 0)
    def _():
        if halves:
            n = w_in[0].shape[0]
            here = pl.multiple_of(at[3] * n, n)
            there = pl.multiple_of((1 - at[3]) * n, n)
            w_o[pl.ds(here, n), :] = w_in[0][...]
            w_o[pl.ds(there, n), :] = w_in[1][...]
        else:
            w_o[...] = w_in[0][...]

    def tile(tok, cot, act):
        pre = lax.dot_general(tok[...], w_o[...], (((1,), (1,)), ((), ())), preferred_element_type=F32)
        k = math.sqrt(2.0 / math.pi)
        square = pre * pre
        t = jnp.tanh(k * (pre + 0.044715 * (pre * square)))
        half = 0.5 * (1.0 + t)
        act[...] = (pre * half).astype(BF)
        slope = half + 0.5 * pre * (1.0 - t * t) * (k * (1.0 + 3 * 0.044715 * square))
        slope = (cot[...].astype(F32) * slope).astype(BF)
        slope_o[...] = slope
        term = lax.dot_general(slope, tok[...], (((0,), (0,)), ((), ())), preferred_element_type=F32)

        @pl.when(i == 0)
        def _():
            acc[...] = term

        @pl.when(i > 0)
        def _():
            acc[...] += term

    @pl.when(i < n_own)
    def _():
        tile(tok_o, cot_o, act_o)

    @pl.when(i >= n_own)
    def _():
        tile(tok_p, cot_p, act_p)

    @pl.when(i == pl.num_programs(0) - 1)
    def _():
        n = keep_o.shape[0]
        keep = pl.multiple_of(at[2] * n, n)
        send = pl.multiple_of((1 - at[2]) * n, n)
        keep_o[...] = (acc[pl.ds(keep, n), :] * scale).astype(BF)
        send_o[...] = (acc[pl.ds(send, n), :] * scale).astype(BF)


def block(role, at, tok_o, tok_p, ws, cot_o, cot_p, bufs, scale):
    m, d = tok_o.shape
    rows = 384
    n_all = cot_p.shape[1]
    n_own = m // TILE
    low = lambda i: jnp.minimum(i, n_own - 1)
    high = lambda i: jnp.maximum(i - n_own, 0)
    w_specs = [pl.BlockSpec(w.shape, lambda i, at: (0, 0)) for w in ws]
    alias_args = [] if bufs is None else list(bufs)
    n_alias = len(alias_args)
    before = 1 + 2 + len(ws) + 2
    out = pl.pallas_call(
        functools.partial(block_kernel, len(ws) == 2, scale, n_alias),
        grid_spec=pltpu.PrefetchScalarGridSpec(
            num_scalar_prefetch=1,
            grid=(2 * n_own,),
            in_specs=[
                pl.BlockSpec((TILE, d), lambda i, at: (low(i), 0)),
                pl.BlockSpec((TILE, d), lambda i, at: (high(i), 0)),
                *w_specs,
                pl.BlockSpec((TILE, rows), lambda i, at: (low(i), at[0])),
                pl.BlockSpec((TILE, rows), lambda i, at: (high(i), at[1])),
                *([pl.BlockSpec(memory_space=pl.ANY)] * n_alias),
            ],
            out_specs=[
                pl.BlockSpec((TILE, rows), lambda i, at: (low(i), at[0])),
                pl.BlockSpec((TILE, rows), lambda i, at: (high(i), at[1])),
                pl.BlockSpec((TILE, rows), lambda i, at: (i, role)),
                pl.BlockSpec((rows, d), lambda i, at: (role, 0)),
                pl.BlockSpec((rows // 2, d), lambda i, at: (0, 0)),
                pl.BlockSpec((rows // 2, d), lambda i, at: (0, 0)),
            ],
            scratch_shapes=[pltpu.VMEM((rows, d), F32)],
        ),
        out_shape=[
            jax.ShapeDtypeStruct((m, 2 * n_all), BF),
            jax.ShapeDtypeStruct((m, n_all), BF),
            jax.ShapeDtypeStruct((2 * m, n_all), BF),
            jax.ShapeDtypeStruct((n_all, d), BF),
            jax.ShapeDtypeStruct((rows // 2, d), BF),
            jax.ShapeDtypeStruct((rows // 2, d), BF),
        ],
        input_output_aliases={before + j: j for j in range(n_alias)},
        compiler_params=pltpu.CompilerParams(
            dimension_semantics=("arbitrary",), vmem_limit_bytes=32 * 1024 * 1024
        ),
        cost_estimate=pl.CostEstimate(
            flops=2 * 2 * 2 * m * rows * d, bytes_accessed=10 * rows * d * 2, transcendentals=2 * m * rows
        ),
        name=f"block_{role}",
    )(at, tok_o, tok_p, *ws, cot_o, cot_p, *alias_args)
    return out[:4], out[4], out[5]


def copy_kernel(at, src, *refs):
    refs[-1][...] = src[...]


def pack(cot, c, rows):
    m, n = cot.shape
    return pl.pallas_call(
        copy_kernel,
        grid_spec=pltpu.PrefetchScalarGridSpec(
            num_scalar_prefetch=1,
            grid=(n // rows // 2,),
            in_specs=[pl.BlockSpec((m, rows), lambda i, at: (0, 2 * i + 1 - at[0]))],
            out_specs=pl.BlockSpec((m, rows), lambda i, at: (0, i)),
        ),
        out_shape=jax.ShapeDtypeStruct((m, n // 2), BF),
        name="pack",
    )(c[None], cot)


def unpack(act, received, c, rows):
    m, n = act.shape
    return pl.pallas_call(
        copy_kernel,
        grid_spec=pltpu.PrefetchScalarGridSpec(
            num_scalar_prefetch=1,
            grid=(n // rows // 2,),
            in_specs=[pl.BlockSpec((m, rows), lambda i, at: (0, i)), pl.BlockSpec(memory_space=pl.ANY)],
            out_specs=pl.BlockSpec((m, rows), lambda i, at: (0, 2 * i + 1 - at[0])),
        ),
        out_shape=jax.ShapeDtypeStruct((m, n), BF),
        input_output_aliases={2: 0},
        name="unpack",
    )(c[None], received, act)


def local(tokens, weight, cotangent):
    rows = weight.shape[0]
    f, r = lax.axis_index("fsdp"), lax.axis_index("rep")
    x, y, zh, zl, c = coords(f, r)
    total_tokens = tokens.shape[0] * lax.axis_size("fsdp") * lax.axis_size("rep")
    scale = 1.0 / math.sqrt(total_tokens)

    own = weight.astype(BF)
    tok_p = other_core(tokens)
    w = {"own": [own]}
    w["a"] = [x_first(own)]
    w["b"] = [x_second(own)]
    cot_p = other_core(pack(cotangent, c, rows))

    def z_gather(v):
        near = z_outer(rows_of(v, 1 - zl, 2))
        return [near, z_inner(near)]

    w["own_z"] = z_gather(own)
    w["ab"] = [x_second(w["a"][0])]
    w["a_z"] = z_gather(w["a"][0])
    w["b_z"] = z_gather(w["b"][0])
    w["ab_z"] = [x_second(v) for v in w["a_z"]]

    xa = jnp.where(c == 0, x ^ 1, 3 - x)
    xb = jnp.where(c == 0, 3 - x, x ^ 1)
    at_x = {"own": x, "a": xa, "b": xb, "ab": (x + 2) % 4}
    y0, y1 = y % 2, y // 2
    y_half = jnp.where(c == 0, y0 ^ y1, y1)
    y_part = jnp.where(c == 0, y1, y0)

    bufs = None
    sums = {}
    for role, name in enumerate(ROLES):
        there = 2 * at_x[name.removesuffix("_z")] + (1 - zh if name.endswith("_z") else zh)
        at = jnp.stack([2 * there + c, there, y_half, zl]).astype(jnp.int32)
        bufs, send, keep = block(role, at, tokens, tok_p, w[name], cotangent, cot_p, bufs, scale)
        half = add(keep, y_first(send))
        sums[name] = add(rows_of(half, y_part, 2), y_second(rows_of(half, 1 - y_part, 2)))
    act, act_p, slope, w_all = bufs

    def x_sum(end):
        got = x_first(jnp.concatenate([sums["a" + end], sums["ab" + end]]))
        n = got.shape[0] // 2
        rest = add(sums["b" + end], got[n:])
        return add(add(sums["own" + end], got[:n]), x_second(rest))

    same, other = x_sum(""), x_sum("_z")
    k = zh ^ zl
    got = z_inner(jnp.concatenate([rows_of(same, 1 - k, 2), rows_of(other, 1 - k, 2)]))
    n = got.shape[0] // 2
    same, other = add(rows_of(same, k, 2), got[:n]), add(rows_of(other, k, 2), got[n:])
    piece = add(same, z_outer(other))

    pair = z_inner(piece)
    quarter = jnp.where(k == 0, jnp.concatenate([piece, pair]), jnp.concatenate([pair, piece]))
    q2 = y_second(quarter)
    half = jnp.where(y_part == 0, jnp.concatenate([quarter, q2]), jnp.concatenate([q2, quarter]))
    h2 = y_first(half)
    weight_grad = jnp.where(y_half == 0, jnp.concatenate([half, h2]), jnp.concatenate([h2, half])).astype(F32)

    activated = unpack(act, other_core(act_p), c, rows)
    grad = jnp.dot(slope, w_all, preferred_element_type=F32)
    m = tokens.shape[0]
    input_grad = grad[:m] + other_core(grad[m:])
    return activated, input_grad, weight_grad


def solution(mesh):
    in_specs = (P(("fsdp", "rep"), None), P("fsdp", None), P(("fsdp", "rep"), None))
    out_specs = (P(("fsdp", "rep"), None), P(("fsdp", "rep"), None), P("fsdp", None))
    return jax.shard_map(local, mesh=mesh, in_specs=in_specs, out_specs=out_specs, check_vma=False)
```

time: 418 us -> 318 us (0.76); the launches traced: 418 us -> 312 us
  waiting for transfers between devices: 343 us -> 114 us
  Pallas kernels: 0 us -> 91.4 us
  starting transfers between devices: 0.3 us -> 62.6 us
  matrix products: 52.9 us -> 12.4 us
  other arithmetic: 5.88 us -> 20.8 us
  between operations: 13.8 us -> 1.26 us
  local copies, waits for them, and re-layouts: 2.64 us -> 9.38 us
    reduce_scatter x1 -> x0, waiting for transfers between devices: 157 us -> none  [local(): lax.psum_scatter((lax.dot_general(slope_grad, tokens, (((0,), (0,)), ((),...]
    all_gather x1 -> x0, waiting for transfers between devices: 123 us -> none  [local(): full_rows = lax.all_gather(weight_b, 'fsdp', axis=0, tiled=True)]
    ppermute x0 -> x40, waiting for transfers between devices: none -> 114 us  [permute(): return lax.ppermute(value, ('fsdp', 'rep'), pairs)]
    pallas_call x0 -> x10, Pallas kernels: none -> 91.4 us  [the longest x8 79.1 us: block(): pl.pallas_call(functools.partial(block_kernel, len(ws) == 2, scale, n_ali...]
    psum x1 -> x0, waiting for transfers between devices: 62.7 us -> none  [local(): weight_grad = lax.psum(shard_grad, 'rep').astype(jnp.float32)]
    ppermute x0 -> x40, starting transfers between devices: none -> 62.6 us  [permute(): return lax.ppermute(value, ('fsdp', 'rep'), pairs)]
    dot_general x3 -> x1, matrix products: 52.9 us -> 12.4 us  [local(): grad = jnp.dot(slope, w_all, preferred_element_type=F32)]
    dynamic_slice x0 -> x13, local copies, waits for them, and re-layouts: none -> 6 us  [rows_of(): return lax.dynamic_slice_in_dim(v, part * n, n, 0)]
  transfers between devices with their start and end apart: 3 -> 40, of which waited for: 3 -> 17; matrix products, arithmetic and copies ran while one was open for 4% -> 12% of each run, Pallas kernels for 0% -> 27%
where the time goes in v1:
time: 318 us; the launch traced here: 312 us
  waiting for transfers between devices  114 us (36%)
  Pallas kernels  91.4 us (29%)
  starting transfers between devices  62.6 us (20%)
  other arithmetic  20.8 us (7%)
  matrix products  12.4 us (4%)
  local copies, waits for them, and re-layouts  9.38 us (3%)
    ppermute x40, waiting for transfers between devices, permute(): return lax.ppermute(value, ('fsdp', 'rep'), pairs)  114 us
    pallas_call x8, Pallas kernels, block(): pl.pallas_call(functools.partial(block_kernel, len(ws) == 2, scale, n_ali...  79.1 us
    ppermute x40, starting transfers between devices, permute(): return lax.ppermute(value, ('fsdp', 'rep'), pairs)  62.6 us
    dot_general x1, matrix products, local(): grad = jnp.dot(slope, w_all, preferred_element_type=F32)  12.4 us
  transfers between devices with their start and end apart: 40, of which 17 were waited for; matrix products, arithmetic and copies ran while one was open for 12% of the time, Pallas kernels for 27%

profile of v1, /device:TPU:0, one launch (start us, length us, event | category | flops | bytes accessed | tf_op | source)
XLA Modules:
  0.0 312.2 jit_solution(7180789311372201737)
XLA Ops:
  0.6 6.2 %pack.1 = bf16[512,3072]{1,0:T(8,128)(2,1)} custom-call(s32[1]{0:T(128)} %bitcast.at, bf16[512,6144]{1,0:T(8,128)(2,1)} %refs_2_.7), custom_call_target="tpu_custom_call" | custom-call | tf_op jit(solution)/shard_map/pack/pallas_call | solution.py:191
  6.8 2.8 convert_element_type.231.refs_0_
  9.6 1.6 collective-permute-start.1
  11.2 2.1 collective-permute-start.7
  13.3 23.8 %collective-permute-done.1.refs_0_ = bf16[384,1536]{1,0:T(8,128)(2,1)} collective-permute-done((bf16[384,1536]{1,0:T(8,128)(2,1)}, bf16[384,1536]{1,0:T(8,128)(2,1)}, u32[]{:S(2)}, u32[]{:S(2)}) %collective-permute-start.1) | collective-permute-done | bytes 1179680 | tf_op jit(solution)/shard_map/ppermute | solution.py:27
  37.0 1.9 constant_dynamic-slice_fusion.12
  39.0 4.0 %collective-permute-start.2 = (bf16[192,1536]{1,0:T(8,128)(2,1)}, bf16[192,1536]{1,0:T(8,128)(2,1)}, u32[]{:S(2)}, u32[]{:S(2)}) collective-permute-start(bf16[192,1536]{1,0:T(8,128)(2,1)} %constant_dynamic-slice_fusion.12), channel_id=1, source_target_pairs={{0,17},{1,16},{2,19},{3,18},{4,21},{5,20},{6,23},{7,22},{8,25},{9,... | collective-permute-start | bytes 1769480 | tf_op jit(solution)/shard_map/ppermute | solution.py:27
  43.0 1.9 constant_dynamic-slice_fusion.10
  45.1 1.9 constant_dynamic-slice_fusion.11
  47.0 3.2 %collective-permute-start.8 = (bf16[192,1536]{1,0:T(8,128)(2,1)}, bf16[192,1536]{1,0:T(8,128)(2,1)}, u32[]{:S(2)}, u32[]{:S(2)}) collective-permute-start(bf16[192,1536]{1,0:T(8,128)(2,1)} %constant_dynamic-slice_fusion.11), channel_id=1, source_target_pairs={{0,17},{1,16},{2,19},{3,18},{4,21},{5,20},{6,23},{7,22},{8,25},{9,... | collective-permute-start | bytes 1769480 | tf_op jit(solution)/shard_map/ppermute | solution.py:27
  50.2 7.3 %collective-permute-done.2.refs_0_ = bf16[192,1536]{1,0:T(8,128)(2,1)} collective-permute-done((bf16[192,1536]{1,0:T(8,128)(2,1)}, bf16[192,1536]{1,0:T(8,128)(2,1)}, u32[]{:S(2)}, u32[]{:S(2)}) %collective-permute-start.2) | collective-permute-done | bytes 589856 | tf_op jit(solution)/shard_map/ppermute | solution.py:27
  57.7 12.4 %collective-permute-done.11.refs_0_ = bf16[192,1536]{1,0:T(8,128)(2,1)} collective-permute-done((bf16[192,1536]{1,0:T(8,128)(2,1)}, bf16[192,1536]{1,0:T(8,128)(2,1)}, u32[]{:S(2)}, u32[]{:S(2)}) %collective-permute-start.11) | collective-permute-done | bytes 589856 | tf_op jit(solution)/shard_map/ppermute | solution.py:27
  70.1 4.3 %collective-permute-start.10 = (bf16[384,1536]{1,0:T(8,128)(2,1)}, bf16[384,1536]{1,0:T(8,128)(2,1)}, u32[]{:S(2)}, u32[]{:S(2)}) collective-permute-start(bf16[384,1536]{1,0:T(8,128)(2,1)} %collective-permute-done.1.refs_0_), channel_id=1, source_target_pairs={{0,96},{1,97},{2,98},{3,99},{4,100},{5,101},{6,102},{7,103},{8,40}... | collective-permute-start | bytes 3538952 | tf_op jit(solution)/shard_map/ppermute | solution.py:27
  74.7 8.0 %collective-permute-done.8.refs_0_ = bf16[192,1536]{1,0:T(8,128)(2,1)} collective-permute-done((bf16[192,1536]{1,0:T(8,128)(2,1)}, bf16[192,1536]{1,0:T(8,128)(2,1)}, u32[]{:S(2)}, u32[]{:S(2)}) %collective-permute-start.8) | collective-permute-done | bytes 589856 | tf_op jit(solution)/shard_map/ppermute | solution.py:27
  82.7 3.4 %collective-permute-start.3 = (bf16[192,1536]{1,0:T(8,128)(2,1)}, bf16[192,1536]{1,0:T(8,128)(2,1)S(1)}, u32[]{:S(2)}, u32[]{:S(2)}) collective-permute-start(bf16[192,1536]{1,0:T(8,128)(2,1)} %collective-permute-done.2.refs_0_), channel_id=1, source_target_pairs={{0,96},{1,97},{2,98},{3,99},{4,100},{5,101},{6,102},{7,103},{8,40}... | collective-permute-start | bytes 1769480 | tf_op jit(solution)/shard_map/ppermute | solution.py:27
  86.8 10.0 %block_0.1 = (bf16[512,6144]{1,0:T(8,128)(2,1)}, bf16[512,3072]{1,0:T(8,128)(2,1)}, bf16[1024,3072]{1,0:T(8,128)(2,1)S(1)}, bf16[3072,1536]{1,0:T(8,128)(2,1)}, ...) custom-call(s32[4]{0:T(128)S(1)} %add_add_fusion.7.at, bf16[512,1536]{1,0:T(8,128)(2,1)} %tok_o.15, ...), custom_call_target="tpu_custom_call" | custom-call | flops 2415919104 | bytes 11796480 | tf_op jit(solution)/shard_map/block_0/pallas_call | solution.py:142
  96.8 10.0 %block_1.1 = (bf16[512,6144]{1,0:T(8,128)(2,1)}, bf16[512,3072]{1,0:T(8,128)(2,1)}, bf16[1024,3072]{1,0:T(8,128)(2,1)S(1)}, bf16[3072,1536]{1,0:T(8,128)(2,1)}, ...) custom-call(s32[4]{0:T(128)S(1)} %add_add_fusion.6.at, ...), custom_call_target="tpu_custom_call", output_to_operand_aliasing={{0}: (6, {}), {1}: (7, {}), {2}: (8, {}), {3}: (9, {})} | custom-call | flops 2415919104 | bytes 11796480 | tf_op jit(solution)/shard_map/block_1/pallas_call | solution.py:142
  106.8 10.0 %block_2.1 = (bf16[512,6144]{1,0:T(8,128)(2,1)}, bf16[512,3072]{1,0:T(8,128)(2,1)}, bf16[1024,3072]{1,0:T(8,128)(2,1)S(1)}, bf16[3072,1536]{1,0:T(8,128)(2,1)}, ...) custom-call(s32[4]{0:T(128)S(1)} %add_add_fusion.5.at, ...), custom_call_target="tpu_custom_call", output_to_operand_aliasing={{0}: (6, {}), {1}: (7, {}), {2}: (8, {}), {3}: (9, {})} | custom-call | flops 2415919104 | bytes 11796480 | tf_op jit(solution)/shard_map/block_2/pallas_call | solution.py:142
  116.8 1.8 collective-permute-start.17
  118.6 9.8 %block_3.1 = (bf16[512,6144]{1,0:T(8,128)(2,1)}, bf16[512,3072]{1,0:T(8,128)(2,1)}, bf16[1024,3072]{1,0:T(8,128)(2,1)S(1)}, bf16[3072,1536]{1,0:T(8,128)(2,1)}, ...) custom-call(s32[4]{0:T(128)S(1)} %add_add_fusion.4.at, ...), custom_call_target="tpu_custom_call", output_to_operand_aliasing={{0}: (7, {}), {1}: (8, {}), {2}: (9, {}), {3}: (10, {})} | custom-call | flops 2415919104 | bytes 11796480 | tf_op jit(solution)/shard_map/block_3/pallas_call | solution.py:142
  128.4 10.0 %block_4.1 = (bf16[512,6144]{1,0:T(8,128)(2,1)}, bf16[512,3072]{1,0:T(8,128)(2,1)}, bf16[1024,3072]{1,0:T(8,128)(2,1)S(1)}, bf16[3072,1536]{1,0:T(8,128)(2,1)}, ...) custom-call(s32[4]{0:T(128)S(1)} %add_add_fusion.3.at, ...), custom_call_target="tpu_custom_call", output_to_operand_aliasing={{0}: (6, {}), {1}: (7, {}), {2}: (8, {}), {3}: (9, {})} | custom-call | flops 2415919104 | bytes 11796480 | tf_op jit(solution)/shard_map/block_4/pallas_call | solution.py:142
  139.0 9.9 %block_5.1 = (bf16[512,6144]{1,0:T(8,128)(2,1)}, bf16[512,3072]{1,0:T(8,128)(2,1)}, bf16[1024,3072]{1,0:T(8,128)(2,1)S(1)}, bf16[3072,1536]{1,0:T(8,128)(2,1)}, ...) custom-call(s32[4]{0:T(128)S(1)} %add_add_fusion.2.at, ...), custom_call_target="tpu_custom_call", output_to_operand_aliasing={{0}: (7, {}), {1}: (8, {}), {2}: (9, {}), {3}: (10, {})} | custom-call | flops 2415919104 | bytes 11796480 | tf_op jit(solution)/shard_map/block_5/pallas_call | solution.py:142
  148.9 1.9 collective-permute-start.22
  150.8 9.9 %block_6.1 = (bf16[512,6144]{1,0:T(8,128)(2,1)}, bf16[512,3072]{1,0:T(8,128)(2,1)}, bf16[1024,3072]{1,0:T(8,128)(2,1)S(1)}, bf16[3072,1536]{1,0:T(8,128)(2,1)}, ...) custom-call(s32[4]{0:T(128)S(1)} %add_add_fusion.1.at, ...), custom_call_target="tpu_custom_call", output_to_operand_aliasing={{0}: (7, {}), {1}: (8, {}), {2}: (9, {}), {3}: (10, {})} | custom-call | flops 2415919104 | bytes 11796480 | tf_op jit(solution)/shard_map/block_6/pallas_call | solution.py:142
  161.2 1.6 collective-permute-start.27
  162.8 9.5 %block_7.1 = (bf16[512,6144]{1,0:T(8,128)(2,1)}, bf16[512,3072]{1,0:T(8,128)(2,1)}, bf16[1024,3072]{1,0:T(8,128)(2,1)S(1)}, bf16[3072,1536]{1,0:T(8,128)(2,1)}, ...) custom-call(s32[4]{0:T(128)S(1)} %add_add_fusion.at, ...), custom_call_target="tpu_custom_call", output_to_operand_aliasing={{0}: (7, {}), {1}: (8, {}), {2}: (9, {}), {3}: (10, {})} | custom-call | flops 2415919104 | bytes 11796480 | tf_op jit(solution)/shard_map/block_7/pallas_call | solution.py:142
  172.3 12.4 %fusion.1 = f32[1024,1536]{1,0:T(8,128)S(1)} fusion(bf16[1024,3072]{1,0:T(8,128)(2,1)S(1)} %get-tuple-element.81, bf16[3072,1536]{1,0:T(8,128)(2,1)} %get-tuple-element.82), kind=kOutput, calls=%fused_computation.54 | convolution fusion | flops 9663676416 | bytes 22020096 | tf_op jit(solution)/shard_map/dot_general | solution.py:282
  185.0 2.5 copy-done
  188.0 1.7 collective-permute-start.32
  190.6 1.1 collective-permute-start.14
  192.2 5.1 %collective-permute-done.29 = bf16[192,1536]{1,0:T(8,128)(2,1)S(1)} collective-permute-done((bf16[192,1536]{1,0:T(8,128)(2,1)S(1)}, bf16[192,1536]{1,0:T(8,128)(2,1)S(1)}, u32[]{:S(2)}, u32[]{:S(2)}) %collective-permute-start.29) | collective-permute-done | bytes 589856 | tf_op jit(solution)/shard_map/ppermute | solution.py:27
  197.3 2.2 collective-permute-start.18
  199.7 7.0 %collective-permute-done.32 = bf16[192,1536]{1,0:T(8,128)(2,1)S(1)} collective-permute-done((bf16[192,1536]{1,0:T(8,128)(2,1)S(1)}, bf16[192,1536]{1,0:T(8,128)(2,1)S(1)}, u32[]{:S(2)}, u32[]{:S(2)}) %collective-permute-start.32) | collective-permute-done | bytes 589856 | tf_op jit(solution)/shard_map/ppermute | solution.py:27
  206.7 2.3 collective-permute-start.20
  209.2 7.1 %collective-permute-done.25 = bf16[192,1536]{1,0:T(8,128)(2,1)S(1)} collective-permute-done((bf16[192,1536]{1,0:T(8,128)(2,1)S(1)}, bf16[192,1536]{1,0:T(8,128)(2,1)S(1)}, u32[]{:S(2)}, u32[]{:S(2)}) %collective-permute-start.25) | collective-permute-done | bytes 589856 | tf_op jit(solution)/shard_map/ppermute | solution.py:27
  216.3 2.2 collective-permute-start.23
  218.7 1.1 collective-permute-start.28
  220.0 2.3 collective-permute-start.30
  222.3 5.0 %collective-permute-done.28 = bf16[96,1536]{1,0:T(8,128)(2,1)S(1)} collective-permute-done((bf16[96,1536]{1,0:T(8,128)(2,1)S(1)}, bf16[96,1536]{1,0:T(8,128)(2,1)S(1)}, u32[]{:S(2)}, u32[]{:S(2)}) %collective-permute-start.28) | collective-permute-done | bytes 294944 | tf_op jit(solution)/shard_map/ppermute | solution.py:27
  227.5 3.1 collective-permute-done.30
  230.8 2.3 collective-permute-start.16
  233.1 4.2 %collective-permute-done.21 = bf16[192,1536]{1,0:T(8,128)(2,1)S(1)} collective-permute-done((bf16[192,1536]{1,0:T(8,128)(2,1)S(1)}, bf16[192,1536]{1,0:T(8,128)(2,1)S(1)}, u32[]{:S(2)}, u32[]{:S(2)}) %collective-permute-start.21) | collective-permute-done | bytes 589856 | tf_op jit(solution)/shard_map/ppermute | solution.py:27
  237.3 2.2 collective-permute-start.33
  239.5 5.6 %collective-permute-done.33 = bf16[96,1536]{1,0:T(8,128)(2,1)S(1)} collective-permute-done((bf16[96,1536]{1,0:T(8,128)(2,1)S(1)}, bf16[96,1536]{1,0:T(8,128)(2,1)S(1)}, u32[]{:S(2)}, u32[]{:S(2)}) %collective-permute-start.33) | collective-permute-done | bytes 294944 | tf_op jit(solution)/shard_map/ppermute | solution.py:27
  245.2 2.2 collective-permute-start.26
  247.4 4.7 %collective-permute-start.24 = (bf16[96,1536]{1,0:T(8,128)(2,1)S(1)}, bf16[96,1536]{1,0:T(8,128)(2,1)S(1)}, u32[]{:S(2)}, u32[]{:S(2)}) collective-permute-start(bf16[96,1536]{1,0:T(8,128)(2,1)S(1)} %add_convert_fusion.16), channel_id=1, source_target_pairs={{0,96},{1,97},{2,98},{3,99},{4,100},{5,101},{6,102},{7,103},{8,40}... | collective-permute-start | bytes 884744 | tf_op jit(solution)/shard_map/ppermute | solution.py:27
  252.2 4.5 %collective-permute-done.24 = bf16[96,1536]{1,0:T(8,128)(2,1)S(1)} collective-permute-done((bf16[96,1536]{1,0:T(8,128)(2,1)S(1)}, bf16[96,1536]{1,0:T(8,128)(2,1)S(1)}, u32[]{:S(2)}, u32[]{:S(2)}) %collective-permute-start.24) | collective-permute-done | bytes 294944 | tf_op jit(solution)/shard_map/ppermute | solution.py:27
  256.9 3.2 %collective-permute-done.34 = bf16[96,1536]{1,0:T(8,128)(2,1)S(1)} collective-permute-done((bf16[96,1536]{1,0:T(8,128)(2,1)S(1)}, bf16[96,1536]{1,0:T(8,128)(2,1)S(1)}, u32[]{:S(2)}, u32[]{:S(2)}) %collective-permute-start.34) | collective-permute-done | bytes 294944 | tf_op jit(solution)/shard_map/ppermute | solution.py:27
  261.0 0.7 pad_maximum_fusion.2
  261.8 3.0 collective-permute-start.35
  264.8 6.1 %collective-permute-done.35 = bf16[96,1536]{1,0:T(8,128)(2,1)} collective-permute-done((bf16[96,1536]{1,0:T(8,128)(2,1)}, bf16[96,1536]{1,0:T(8,128)(2,1)}, u32[]{:S(2)}, u32[]{:S(2)}) %collective-permute-start.35) | collective-permute-done | bytes 294944 | tf_op jit(solution)/shard_map/ppermute | solution.py:27
  270.9 1.0 add_convert_fusion.23
  272.0 3.5 %collective-permute-start.36 = (bf16[48,1536]{1,0:T(8,128)(2,1)S(1)}, bf16[48,1536]{1,0:T(8,128)(2,1)S(1)}, u32[]{:S(2)}, u32[]{:S(2)}) collective-permute-start(bf16[48,1536]{1,0:T(8,128)(2,1)S(1)} %add_convert_fusion.23), channel_id=1, source_target_pairs={{0,17},{1,16},{2,19},{3,18},{4,21},{5,20},{6,23},{7,22},{8,25},{9,... | collective-permute-start | bytes 442376 | tf_op jit(solution)/shard_map/ppermute | solution.py:27
  275.5 3.1 %collective-permute-done.36 = bf16[48,1536]{1,0:T(8,128)(2,1)S(1)} collective-permute-done((bf16[48,1536]{1,0:T(8,128)(2,1)S(1)}, bf16[48,1536]{1,0:T(8,128)(2,1)S(1)}, u32[]{:S(2)}, u32[]{:S(2)}) %collective-permute-start.36) | collective-permute-done | bytes 147488 | tf_op jit(solution)/shard_map/ppermute | solution.py:27
  278.6 1.6 add_convert_fusion.22
  280.2 1.8 collective-permute-start.37
  282.0 3.7 %collective-permute-done.37 = bf16[48,1536]{1,0:T(8,128)(2,1)} collective-permute-done((bf16[48,1536]{1,0:T(8,128)(2,1)}, bf16[48,1536]{1,0:T(8,128)(2,1)}, u32[]{:S(2)}, u32[]{:S(2)}) %collective-permute-start.37) | collective-permute-done | bytes 147488 | tf_op jit(solution)/shard_map/ppermute | solution.py:27
  285.7 1.2 maximum_select_fusion.2
  286.9 3.1 collective-permute-start.38
  290.0 5.1 %collective-permute-done.38 = bf16[96,1536]{1,0:T(8,128)(2,1)} collective-permute-done((bf16[96,1536]{1,0:T(8,128)(2,1)S(1)}, bf16[96,1536]{1,0:T(8,128)(2,1)}, u32[]{:S(2)}, u32[]{:S(2)}) %collective-permute-start.38) | collective-permute-done | bytes 294944 | tf_op jit(solution)/shard_map/ppermute | solution.py:27
  295.0 2.0 maximum_select_fusion.1
  297.2 6.1 %unpack.1 = bf16[512,6144]{1,0:T(8,128)(2,1)} custom-call(s32[1]{0:T(128)} %bitcast.at, bf16[512,3072]{1,0:T(8,128)(2,1)} %collective-permute-done.13.src, bf16[512,6144]{1,0:T(8,128)(2,1)} %get-tuple-element.80.refs_0_), custom_call_target="tpu_custom_call", output_to_operand_aliasing={{}: (2, {})} | custom-call | tf_op jit(solution)/shard_map/unpack/pallas_call | solution.py:206
  303.4 5.1 %slice_add_fusion = f32[512,1536]{1,0:T(8,128)} fusion(f32[512,1536]{1,0:T(8,128)} %collective-permute-done.14, f32[1024,1536]{1,0:T(8,128)} %copy-done), kind=kLoop, calls=%fused_computation | loop fusion | flops 786432 | bytes 9437184 | tf_op jit(solution)/shard_map/add | solution.py:284
  308.5 3.5 %fusion = f32[384,1536]{1,0:T(8,128)} fusion(bf16[192,1536]{1,0:T(8,128)(2,1)} %collective-permute-done.39, bf16[192,1536]{1,0:T(8,128)(2,1)} %maximum_select_fusion.1, pred[]{:T(512)S(6)} %eq.22), kind=kLoop, calls=%fused_computation.2 | loop fusion | flops 5898240 | bytes 3538945 | tf_op jit(solution)/shard_map/convert_element_type | solution.py:279
  (79 shorter events, 7.1 us)
Async XLA Ops:
  6.8 79.4 %collective-permute-start.6 = (bf16[512,3072]{1,0:T(8,128)(2,1)}, bf16[512,3072]{1,0:T(8,128)(2,1)S(1)}, u32[]{:S(2)}, u32[]{:S(2)}) collective-permute-start(bf16[512,3072]{1,0:T(8,128)(2,1)} %pack.1), channel_id=1, source_target_pairs={{0,8},{1,9},{2,10},{3,11},{4,12},{5,13},{6,14},{7,15},{8,0},{9,1},... | collective-permute-start | bytes 9437192 | tf_op jit(solution)/shard_map/ppermute | solution.py:27
  9.6 27.4 %collective-permute-start.1 = (bf16[384,1536]{1,0:T(8,128)(2,1)}, bf16[384,1536]{1,0:T(8,128)(2,1)}, u32[]{:S(2)}, u32[]{:S(2)}) collective-permute-start(bf16[384,1536]{1,0:T(8,128)(2,1)} %convert_element_type.231.refs_0_), channel_id=1, source_target_pairs={{0,32},{1,33},{2,34},{3,35},{4,36},{5,37},{6,38},{7,39},{8,104},{9... | collective-permute-start | bytes 3538952 | tf_op jit(solution)/shard_map/ppermute | solution.py:27
  11.2 33.9 %collective-permute-start.7 = (bf16[384,1536]{1,0:T(8,128)(2,1)}, bf16[384,1536]{1,0:T(8,128)(2,1)}, u32[]{:S(2)}, u32[]{:S(2)}) collective-permute-start(bf16[384,1536]{1,0:T(8,128)(2,1)} %convert_element_type.231.refs_0_), channel_id=1, source_target_pairs={{0,96},{1,97},{2,98},{3,99},{4,100},{5,101},{6,102},{7,103},{8,40}... | collective-permute-start | bytes 3538952 | tf_op jit(solution)/shard_map/ppermute | solution.py:27
  13.3 61.4 %collective-permute-start = (bf16[512,1536]{1,0:T(8,128)(2,1)}, bf16[512,1536]{1,0:T(8,128)(2,1)}, u32[]{:S(2)}, u32[]{:S(2)}) collective-permute-start(bf16[512,1536]{1,0:T(8,128)(2,1)} %tok_o.15), channel_id=1, source_target_pairs={{0,8},{1,9},{2,10},{3,11},{4,12},{5,13},{6,14},{7,15},{8,0},{9,1},... | collective-permute-start | bytes 4718600 | tf_op jit(solution)/shard_map/ppermute | solution.py:27
  39.0 18.5 %collective-permute-start.2 = (bf16[192,1536]{1,0:T(8,128)(2,1)}, bf16[192,1536]{1,0:T(8,128)(2,1)}, u32[]{:S(2)}, u32[]{:S(2)}) collective-permute-start(bf16[192,1536]{1,0:T(8,128)(2,1)} %constant_dynamic-slice_fusion.12), channel_id=1, source_target_pairs={{0,17},{1,16},{2,19},{3,18},{4,21},{5,20},{6,23},{7,22},{8,25},{9,... | collective-permute-start | bytes 1769480 | tf_op jit(solution)/shard_map/ppermute | solution.py:27
  44.9 25.2 %collective-permute-start.11 = (bf16[192,1536]{1,0:T(8,128)(2,1)}, bf16[192,1536]{1,0:T(8,128)(2,1)}, u32[]{:S(2)}, u32[]{:S(2)}) collective-permute-start(bf16[192,1536]{1,0:T(8,128)(2,1)} %constant_dynamic-slice_fusion.10), channel_id=1, source_target_pairs={{0,17},{1,16},{2,19},{3,18},{4,21},{5,20},{6,23},{7,22},{8,25},{9,... | collective-permute-start | bytes 1769480 | tf_op jit(solution)/shard_map/ppermute | solution.py:27
  47.0 35.8 %collective-permute-start.8 = (bf16[192,1536]{1,0:T(8,128)(2,1)}, bf16[192,1536]{1,0:T(8,128)(2,1)}, u32[]{:S(2)}, u32[]{:S(2)}) collective-permute-start(bf16[192,1536]{1,0:T(8,128)(2,1)} %constant_dynamic-slice_fusion.11), channel_id=1, source_target_pairs={{0,17},{1,16},{2,19},{3,18},{4,21},{5,20},{6,23},{7,22},{8,25},{9,... | collective-permute-start | bytes 1769480 | tf_op jit(solution)/shard_map/ppermute | solution.py:27
  57.5 28.7 %collective-permute-start.4 = (bf16[192,1536]{1,0:T(8,128)(2,1)}, bf16[192,1536]{1,0:T(8,128)(2,1)}, u32[]{:S(2)}, u32[]{:S(2)}) collective-permute-start(bf16[192,1536]{1,0:T(8,128)(2,1)} %collective-permute-done.2.refs_0_), channel_id=1, source_target_pairs={{0,1},{1,0},{2,3},{3,2},{4,5},{5,4},{6,7},{7,6},{8,9},{9,8},{10,11... | collective-permute-start | bytes 1769480 | tf_op jit(solution)/shard_map/ppermute | solution.py:27
  70.1 58.3 %collective-permute-start.10 = (bf16[384,1536]{1,0:T(8,128)(2,1)}, bf16[384,1536]{1,0:T(8,128)(2,1)}, u32[]{:S(2)}, u32[]{:S(2)}) collective-permute-start(bf16[384,1536]{1,0:T(8,128)(2,1)} %collective-permute-done.1.refs_0_), channel_id=1, source_target_pairs={{0,96},{1,97},{2,98},{3,99},{4,100},{5,101},{6,102},{7,103},{8,40}... | collective-permute-start | bytes 3538952 | tf_op jit(solution)/shard_map/ppermute | solution.py:27
  74.7 42.1 %collective-permute-start.12 = (bf16[192,1536]{1,0:T(8,128)(2,1)}, bf16[192,1536]{1,0:T(8,128)(2,1)S(1)}, u32[]{:S(2)}, u32[]{:S(2)}) collective-permute-start(bf16[192,1536]{1,0:T(8,128)(2,1)} %collective-permute-done.11.refs_0_), channel_id=1, source_target_pairs={{0,1},{1,0},{2,3},{3,2},{4,5},{5,4},{6,7},{7,6},{8,9},{9,8},{10,11... | collective-permute-start | bytes 1769480 | tf_op jit(solution)/shard_map/ppermute | solution.py:27
  82.7 77.9 %collective-permute-start.3 = (bf16[192,1536]{1,0:T(8,128)(2,1)}, bf16[192,1536]{1,0:T(8,128)(2,1)S(1)}, u32[]{:S(2)}, u32[]{:S(2)}) collective-permute-start(bf16[192,1536]{1,0:T(8,128)(2,1)} %collective-permute-done.2.refs_0_), channel_id=1, source_target_pairs={{0,96},{1,97},{2,98},{3,99},{4,100},{5,101},{6,102},{7,103},{8,40}... | collective-permute-start | bytes 1769480 | tf_op jit(solution)/shard_map/ppermute | solution.py:27
  86.2 62.7 %collective-permute-start.9 = (bf16[192,1536]{1,0:T(8,128)(2,1)}, bf16[192,1536]{1,0:T(8,128)(2,1)S(1)}, u32[]{:S(2)}, u32[]{:S(2)}) collective-permute-start(bf16[192,1536]{1,0:T(8,128)(2,1)} %collective-permute-done.8.refs_0_), channel_id=1, source_target_pairs={{0,1},{1,0},{2,3},{3,2},{4,5},{5,4},{6,7},{7,6},{8,9},{9,8},{10,11... | collective-permute-start | bytes 1769480 | tf_op jit(solution)/shard_map/ppermute | solution.py:27
  86.2 75.0 %collective-permute-start.5 = (bf16[192,1536]{1,0:T(8,128)(2,1)}, bf16[192,1536]{1,0:T(8,128)(2,1)S(1)}, u32[]{:S(2)}, u32[]{:S(2)}) collective-permute-start(bf16[192,1536]{1,0:T(8,128)(2,1)} %collective-permute-done.4.refs_1_), channel_id=1, source_target_pairs={{0,96},{1,97},{2,98},{3,99},{4,100},{5,101},{6,102},{7,103},{8,40}... | collective-permute-start | bytes 1769480 | tf_op jit(solution)/shard_map/ppermute | solution.py:27
  116.8 70.6 %collective-permute-start.17 = (bf16[192,1536]{1,0:T(8,128)(2,1)S(1)}, bf16[192,1536]{1,0:T(8,128)(2,1)S(1)}, u32[]{:S(2)}, u32[]{:S(2)}) collective-permute-start(bf16[192,1536]{1,0:T(8,128)(2,1)S(1)} %get-tuple-element.86), channel_id=1, source_target_pairs={{0,2},{1,3},{2,0},{3,1},{4,6},{5,7},{6,4},{7,5},{8,14},{9,15},{10,... | collective-permute-start | bytes 1769480 | tf_op jit(solution)/shard_map/ppermute | solution.py:27
  138.4 49.6 %collective-permute-start.19 = (bf16[192,1536]{1,0:T(8,128)(2,1)S(1)}, bf16[192,1536]{1,0:T(8,128)(2,1)S(1)}, u32[]{:S(2)}, u32[]{:S(2)}) collective-permute-start(bf16[192,1536]{1,0:T(8,128)(2,1)S(1)} %get-tuple-element.88), channel_id=1, source_target_pairs={{0,2},{1,3},{2,0},{3,1},{4,6},{5,7},{6,4},{7,5},{8,14},{9,15},{10,... | collective-permute-start | bytes 1769480 | tf_op jit(solution)/shard_map/ppermute | solution.py:27
  148.9 40.9 %collective-permute-start.22 = (bf16[192,1536]{1,0:T(8,128)(2,1)S(1)}, bf16[192,1536]{1,0:T(8,128)(2,1)S(1)}, u32[]{:S(2)}, u32[]{:S(2)}) collective-permute-start(bf16[192,1536]{1,0:T(8,128)(2,1)S(1)} %get-tuple-element.90), channel_id=1, source_target_pairs={{0,2},{1,3},{2,0},{3,1},{4,6},{5,7},{6,4},{7,5},{8,14},{9,15},{10,... | collective-permute-start | bytes 1769480 | tf_op jit(solution)/shard_map/ppermute | solution.py:27
  160.6 29.9 %collective-permute-start.15 = (bf16[192,1536]{1,0:T(8,128)(2,1)S(1)}, bf16[192,1536]{1,0:T(8,128)(2,1)S(1)}, u32[]{:S(2)}, u32[]{:S(2)}) collective-permute-start(bf16[192,1536]{1,0:T(8,128)(2,1)S(1)} %get-tuple-element.84), channel_id=1, source_target_pairs={{0,2},{1,3},{2,0},{3,1},{4,6},{5,7},{6,4},{7,5},{8,14},{9,15},{10,... | collective-permute-start | bytes 1769480 | tf_op jit(solution)/shard_map/ppermute | solution.py:27
  161.2 30.8 %collective-permute-start.27 = (bf16[192,1536]{1,0:T(8,128)(2,1)S(1)}, bf16[192,1536]{1,0:T(8,128)(2,1)S(1)}, u32[]{:S(2)}, u32[]{:S(2)}) collective-permute-start(bf16[192,1536]{1,0:T(8,128)(2,1)S(1)} %get-tuple-element.94), channel_id=1, source_target_pairs={{0,2},{1,3},{2,0},{3,1},{4,6},{5,7},{6,4},{7,5},{8,14},{9,15},{10,... | collective-permute-start | bytes 1769480 | tf_op jit(solution)/shard_map/ppermute | solution.py:27
  184.7 2.7 copy-start
  187.4 9.9 %collective-permute-start.29 = (bf16[192,1536]{1,0:T(8,128)(2,1)S(1)}, bf16[192,1536]{1,0:T(8,128)(2,1)S(1)}, u32[]{:S(2)}, u32[]{:S(2)}) collective-permute-start(bf16[192,1536]{1,0:T(8,128)(2,1)S(1)} %get-tuple-element.96), channel_id=1, source_target_pairs={{0,2},{1,3},{2,0},{3,1},{4,6},{5,7},{6,4},{7,5},{8,14},{9,15},{10,... | collective-permute-start | bytes 1769480 | tf_op jit(solution)/shard_map/ppermute | solution.py:27
  188.0 18.7 %collective-permute-start.32 = (bf16[192,1536]{1,0:T(8,128)(2,1)S(1)}, bf16[192,1536]{1,0:T(8,128)(2,1)S(1)}, u32[]{:S(2)}, u32[]{:S(2)}) collective-permute-start(bf16[192,1536]{1,0:T(8,128)(2,1)S(1)} %get-tuple-element.98), channel_id=1, source_target_pairs={{0,2},{1,3},{2,0},{3,1},{4,6},{5,7},{6,4},{7,5},{8,14},{9,15},{10,... | collective-permute-start | bytes 1769480 | tf_op jit(solution)/shard_map/ppermute | solution.py:27
  189.9 26.4 %collective-permute-start.25 = (bf16[192,1536]{1,0:T(8,128)(2,1)S(1)}, bf16[192,1536]{1,0:T(8,128)(2,1)S(1)}, u32[]{:S(2)}, u32[]{:S(2)}) collective-permute-start(bf16[192,1536]{1,0:T(8,128)(2,1)S(1)} %get-tuple-element.92), channel_id=1, source_target_pairs={{0,2},{1,3},{2,0},{3,1},{4,6},{5,7},{6,4},{7,5},{8,14},{9,15},{10,... | collective-permute-start | bytes 1769480 | tf_op jit(solution)/shard_map/ppermute | solution.py:27
  190.6 112.8 %collective-permute-start.14 = (f32[512,1536]{1,0:T(8,128)S(1)}, f32[512,1536]{1,0:T(8,128)}, u32[]{:S(2)}, u32[]{:S(2)}) collective-permute-start(f32[512,1536]{1,0:T(8,128)S(1)} %slice.33), channel_id=1, source_target_pairs={{0,8},{1,9},{2,10},{3,11},{4,12},{5,13},{6,14},{7,15},{8,0},{9,1},... | collective-permute-start | bytes 9437192 | tf_op jit(solution)/shard_map/ppermute | solution.py:27
  192.0 105.2 %collective-permute-start.13 = (bf16[512,3072]{1,0:T(8,128)(2,1)}, bf16[512,3072]{1,0:T(8,128)(2,1)}, u32[]{:S(2)}, u32[]{:S(2)}) collective-permute-start(bf16[512,3072]{1,0:T(8,128)(2,1)} %get-tuple-element.79), channel_id=1, source_target_pairs={{0,8},{1,9},{2,10},{3,11},{4,12},{5,13},{6,14},{7,15},{8,0},{9,1},... | collective-permute-start | bytes 9437192 | tf_op jit(solution)/shard_map/ppermute | solution.py:27
  197.3 21.4 %collective-permute-start.18 = (bf16[96,1536]{1,0:T(8,128)(2,1)S(1)}, bf16[96,1536]{1,0:T(8,128)(2,1)S(1)}, u32[]{:S(2)}, u32[]{:S(2)}) collective-permute-start(bf16[96,1536]{1,0:T(8,128)(2,1)S(1)} %constant_dynamic-slice_fusion.8), channel_id=1, source_target_pairs={{0,6},{1,7},{2,4},{3,5},{4,2},{5,3},{6,0},{7,1},{8,10},{9,11},{10,... | collective-permute-start | bytes 884744 | tf_op jit(solution)/shard_map/ppermute | solution.py:27
  206.7 13.2 %collective-permute-start.20 = (bf16[96,1536]{1,0:T(8,128)(2,1)S(1)}, bf16[96,1536]{1,0:T(8,128)(2,1)S(1)}, u32[]{:S(2)}, u32[]{:S(2)}) collective-permute-start(bf16[96,1536]{1,0:T(8,128)(2,1)S(1)} %constant_dynamic-slice_fusion.7), channel_id=1, source_target_pairs={{0,6},{1,7},{2,4},{3,5},{4,2},{5,3},{6,0},{7,1},{8,10},{9,11},{10,... | collective-permute-start | bytes 884744 | tf_op jit(solution)/shard_map/ppermute | solution.py:27
  216.3 14.5 %collective-permute-start.23 = (bf16[96,1536]{1,0:T(8,128)(2,1)S(1)}, bf16[96,1536]{1,0:T(8,128)(2,1)S(1)}, u32[]{:S(2)}, u32[]{:S(2)}) collective-permute-start(bf16[96,1536]{1,0:T(8,128)(2,1)S(1)} %constant_dynamic-slice_fusion.6), channel_id=1, source_target_pairs={{0,6},{1,7},{2,4},{3,5},{4,2},{5,3},{6,0},{7,1},{8,10},{9,11},{10,... | collective-permute-start | bytes 884744 | tf_op jit(solution)/shard_map/ppermute | solution.py:27
  218.7 8.6 %collective-permute-start.28 = (bf16[96,1536]{1,0:T(8,128)(2,1)S(1)}, bf16[96,1536]{1,0:T(8,128)(2,1)S(1)}, u32[]{:S(2)}, u32[]{:S(2)}) collective-permute-start(bf16[96,1536]{1,0:T(8,128)(2,1)S(1)} %constant_dynamic-slice_fusion.3), channel_id=1, source_target_pairs={{0,6},{1,7},{2,4},{3,5},{4,2},{5,3},{6,0},{7,1},{8,10},{9,11},{10,... | collective-permute-start | bytes 884744 | tf_op jit(solution)/shard_map/ppermute | solution.py:27
  220.0 10.6 %collective-permute-start.30 = (bf16[96,1536]{1,0:T(8,128)(2,1)S(1)}, bf16[96,1536]{1,0:T(8,128)(2,1)S(1)}, u32[]{:S(2)}, u32[]{:S(2)}) collective-permute-start(bf16[96,1536]{1,0:T(8,128)(2,1)S(1)} %constant_dynamic-slice_fusion.2), channel_id=1, source_target_pairs={{0,6},{1,7},{2,4},{3,5},{4,2},{5,3},{6,0},{7,1},{8,10},{9,11},{10,... | collective-permute-start | bytes 884744 | tf_op jit(solution)/shard_map/ppermute | solution.py:27
  227.4 9.9 %collective-permute-start.21 = (bf16[192,1536]{1,0:T(8,128)(2,1)S(1)}, bf16[192,1536]{1,0:T(8,128)(2,1)S(1)}, u32[]{:S(2)}, u32[]{:S(2)}) collective-permute-start(bf16[192,1536]{1,0:T(8,128)(2,1)S(1)} %pad_maximum_fusion), channel_id=1, source_target_pairs={{0,32},{1,33},{2,34},{3,35},{4,36},{5,37},{6,38},{7,39},{8,104},{9... | collective-permute-start | bytes 1769480 | tf_op jit(solution)/shard_map/ppermute | solution.py:27
  230.7 16.7 %collective-permute-start.31 = (bf16[192,1536]{1,0:T(8,128)(2,1)S(1)}, bf16[192,1536]{1,0:T(8,128)(2,1)S(1)}, u32[]{:S(2)}, u32[]{:S(2)}) collective-permute-start(bf16[192,1536]{1,0:T(8,128)(2,1)S(1)} %pad_maximum_fusion.1), channel_id=1, source_target_pairs={{0,32},{1,33},{2,34},{3,35},{4,36},{5,37},{6,38},{7,39},{8,104},{9... | collective-permute-start | bytes 1769480 | tf_op jit(solution)/shard_map/ppermute | solution.py:27
  230.8 21.3 %collective-permute-start.16 = (bf16[96,1536]{1,0:T(8,128)(2,1)S(1)}, bf16[96,1536]{1,0:T(8,128)(2,1)S(1)}, u32[]{:S(2)}, u32[]{:S(2)}) collective-permute-start(bf16[96,1536]{1,0:T(8,128)(2,1)S(1)} %constant_dynamic-slice_fusion.9), channel_id=1, source_target_pairs={{0,6},{1,7},{2,4},{3,5},{4,2},{5,3},{6,0},{7,1},{8,10},{9,11},{10,... | collective-permute-start | bytes 884744 | tf_op jit(solution)/shard_map/ppermute | solution.py:27
  237.3 7.9 %collective-permute-start.33 = (bf16[96,1536]{1,0:T(8,128)(2,1)S(1)}, bf16[96,1536]{1,0:T(8,128)(2,1)S(1)}, u32[]{:S(2)}, u32[]{:S(2)}) collective-permute-start(bf16[96,1536]{1,0:T(8,128)(2,1)S(1)} %constant_dynamic-slice_fusion.1), channel_id=1, source_target_pairs={{0,6},{1,7},{2,4},{3,5},{4,2},{5,3},{6,0},{7,1},{8,10},{9,11},{10,... | collective-permute-start | bytes 884744 | tf_op jit(solution)/shard_map/ppermute | solution.py:27
  245.2 11.7 %collective-permute-start.26 = (bf16[96,1536]{1,0:T(8,128)(2,1)S(1)}, bf16[96,1536]{1,0:T(8,128)(2,1)S(1)}, u32[]{:S(2)}, u32[]{:S(2)}) collective-permute-start(bf16[96,1536]{1,0:T(8,128)(2,1)S(1)} %constant_dynamic-slice_fusion.4), channel_id=1, source_target_pairs={{0,6},{1,7},{2,4},{3,5},{4,2},{5,3},{6,0},{7,1},{8,10},{9,11},{10,... | collective-permute-start | bytes 884744 | tf_op jit(solution)/shard_map/ppermute | solution.py:27
  247.4 9.4 %collective-permute-start.24 = (bf16[96,1536]{1,0:T(8,128)(2,1)S(1)}, bf16[96,1536]{1,0:T(8,128)(2,1)S(1)}, u32[]{:S(2)}, u32[]{:S(2)}) collective-permute-start(bf16[96,1536]{1,0:T(8,128)(2,1)S(1)} %add_convert_fusion.16), channel_id=1, source_target_pairs={{0,96},{1,97},{2,98},{3,99},{4,100},{5,101},{6,102},{7,103},{8,40}... | collective-permute-start | bytes 884744 | tf_op jit(solution)/shard_map/ppermute | solution.py:27
  252.1 8.0 %collective-permute-start.34 = (bf16[96,1536]{1,0:T(8,128)(2,1)S(1)}, bf16[96,1536]{1,0:T(8,128)(2,1)S(1)}, u32[]{:S(2)}, u32[]{:S(2)}) collective-permute-start(bf16[96,1536]{1,0:T(8,128)(2,1)S(1)} %add_convert_fusion.9), channel_id=1, source_target_pairs={{0,96},{1,97},{2,98},{3,99},{4,100},{5,101},{6,102},{7,103},{8,40}... | collective-permute-start | bytes 884744 | tf_op jit(solution)/shard_map/ppermute | solution.py:27
  260.3 0.7 copy-start.1
  261.8 9.2 %collective-permute-start.35 = (bf16[96,1536]{1,0:T(8,128)(2,1)}, bf16[96,1536]{1,0:T(8,128)(2,1)}, u32[]{:S(2)}, u32[]{:S(2)}) collective-permute-start(bf16[96,1536]{1,0:T(8,128)(2,1)} %pad_maximum_fusion.2), channel_id=1, source_target_pairs={{0,1},{1,0},{2,3},{3,2},{4,5},{5,4},{6,7},{7,6},{8,9},{9,8},{10,11... | collective-permute-start | bytes 884744 | tf_op jit(solution)/shard_map/ppermute | solution.py:27
  272.0 6.7 %collective-permute-start.36 = (bf16[48,1536]{1,0:T(8,128)(2,1)S(1)}, bf16[48,1536]{1,0:T(8,128)(2,1)S(1)}, u32[]{:S(2)}, u32[]{:S(2)}) collective-permute-start(bf16[48,1536]{1,0:T(8,128)(2,1)S(1)} %add_convert_fusion.23), channel_id=1, source_target_pairs={{0,17},{1,16},{2,19},{3,18},{4,21},{5,20},{6,23},{7,22},{8,25},{9,... | collective-permute-start | bytes 442376 | tf_op jit(solution)/shard_map/ppermute | solution.py:27
  280.2 5.5 %collective-permute-start.37 = (bf16[48,1536]{1,0:T(8,128)(2,1)}, bf16[48,1536]{1,0:T(8,128)(2,1)}, u32[]{:S(2)}, u32[]{:S(2)}) collective-permute-start(bf16[48,1536]{1,0:T(8,128)(2,1)} %add_convert_fusion.22), channel_id=1, source_target_pairs={{0,1},{1,0},{2,3},{3,2},{4,5},{5,4},{6,7},{7,6},{8,9},{9,8},{10,11... | collective-permute-start | bytes 442376 | tf_op jit(solution)/shard_map/ppermute | solution.py:27
  286.9 8.1 %collective-permute-start.38 = (bf16[96,1536]{1,0:T(8,128)(2,1)S(1)}, bf16[96,1536]{1,0:T(8,128)(2,1)}, u32[]{:S(2)}, u32[]{:S(2)}) collective-permute-start(bf16[96,1536]{1,0:T(8,128)(2,1)S(1)} %maximum_select_fusion.2), channel_id=1, source_target_pairs={{0,6},{1,7},{2,4},{3,5},{4,2},{5,3},{6,0},{7,1},{8,10},{9,11},{10,... | collective-permute-start | bytes 884744 | tf_op jit(solution)/shard_map/ppermute | solution.py:27
  297.1 11.4 %collective-permute-start.39 = (bf16[192,1536]{1,0:T(8,128)(2,1)}, bf16[192,1536]{1,0:T(8,128)(2,1)}, u32[]{:S(2)}, u32[]{:S(2)}) collective-permute-start(bf16[192,1536]{1,0:T(8,128)(2,1)} %maximum_select_fusion.1), channel_id=1, source_target_pairs={{0,2},{1,3},{2,0},{3,1},{4,6},{5,7},{6,4},{7,5},{8,14},{9,15},{10,... | collective-permute-start | bytes 1769480 | tf_op jit(solution)/shard_map/ppermute | solution.py:27
